TPU v7x, 32 devices: a whole 2x2x4 slice. The times are simulated.
32 devices in a mesh: row: 2 (over x), col: 16 (over z, y, core).
Axes of the slice: x: 2, y: 2, z: 4, core: 2. Of those that a mesh axis runs over, the one named last changes fastest.
Arguments:
- object_field: float32 [2, 512, 4096], P(None, 'row', 'col'), may hold values from -6 to 6
- probe: float32 [2, 4, 128, 128], replicated, may hold values from -6 to 6
- patterns: bfloat16 [2, 16, 8, 128, 128], P('row', 'col'), may hold values from 0.5 to 2
- row_scales: float32 [2, 16, 8, 128], P('row', 'col'), may hold values from 0.3 to 3
- positions: int32 [2, 16, 8, 2], P('row', 'col'), may hold values from 0 to 255
- counts: int32 [2, 16], P('row', 'col'), may hold values from 4 to 8, as said below
Outputs:
- object_out: float32 [2, 512, 4096], P(None, 'row', 'col')
- probe_out: float32 [2, 4, 128, 128], replicated
Inputs may be any that keep to these rules, and one draw needn't show every extreme that they name: positions p >= counts[a,b] of tile (a,b) are ignored; some tile has all 8 positions live.
All inputs are finite; a program needn't handle non-finite values.
Results may differ from a plain program's by a relative error of at most 0.0003.
Values sent between devices are 32-bit elements; how exact they have to be, the bound alone decides.
A program may use at most 128 MiB of HBM per device.

v0:
```python
import functools
import math

import jax
import jax.numpy as jnp
import numpy as np
from jax import lax
from jax.experimental import pallas as pl
from jax.experimental.pallas import tpu as pltpu
from jax.sharding import PartitionSpec as P

PASSES = 2
TOGETHER = 2
MESH = pl.DeviceIdType.MESH
VMEM = pl.BlockSpec(memory_space=pltpu.VMEM)
SMEM = pl.BlockSpec(memory_space=pltpu.SMEM)
LIMIT = 48 * 1024 * 1024


def dft_tables(length):
    index = np.arange(length)
    angle = (index[:, None] * index[None, :] % length) * (2.0 * math.pi / length)
    cosine, sine = np.cos(angle), np.sin(angle)
    forward = np.block([[cosine, -sine], [sine, cosine]]).astype(np.float32)
    inverse = np.block([[cosine, sine], [-sine, cosine]]).astype(np.float32)
    rights, lefts = [], []
    for table in (forward, inverse):
        high = table.astype(jnp.bfloat16)
        low = (table - high.astype(np.float32)).astype(jnp.bfloat16)
        rights.append(np.concatenate([high, high, low], 0))
        lefts.append(np.concatenate([high, high, low], 1))
    return rights + lefts


def split(value, axis):
    high = value.astype(jnp.bfloat16)
    low = (value - high.astype(jnp.float32)).astype(jnp.bfloat16)
    return jnp.concatenate([high, low, high], axis)


def times_table(value, table):
    return jnp.dot(split(value, 1), table[...], preferred_element_type=jnp.float32)


def table_times(table, value):
    return jnp.dot(table[...], split(value, 0), preferred_element_type=jnp.float32)


def pass_kernel(
    pos, count, ext, probe, amp, fwd_right, inv_right, fwd_left, inv_left, upd, sums, power, far, wave
):
    modes, pix = probe.shape[1], probe.shape[2]
    group = 2 if modes % 2 == 0 else 1
    firsts = range(0, modes, group)
    together = wave.shape[0]
    last = pos.shape[0] - 1
    tall = pix + 8
    upd[...] = jnp.zeros_like(upd)
    sums[...] = jnp.zeros_like(sums)
    power[...] = jnp.sum(probe[0] * probe[0] + probe[1] * probe[1], axis=0)

    def body(step, carry):
        at = [jnp.minimum(step * together + k, last) for k in range(together)]
        places = []
        for k, p in enumerate(at):
            row, col = pos[p, 0], pos[p, 1]
            shift, down = lax.rem(col, pix), lax.rem(row, 8)
            rows = pl.ds(pl.multiple_of(row // 8 * 8, 8), tall)
            lanes = pl.ds(pl.multiple_of(col // pix * pix, pix), 2 * pix)
            places.append((rows, lanes, shift, down))
            live = jnp.where(step * together + k < count[0, 0], 1.0, 0.0).astype(jnp.float32)
            for plane in range(2):
                moved = pltpu.roll(ext[plane, rows, lanes], lax.rem(2 * pix - shift, 2 * pix), 1)
                moved = pltpu.roll(moved[:, :pix], lax.rem(tall - down, tall), 0)[:pix]
                wave[k, plane] = moved * live
        halves, intensity = {}, [None] * together
        for first in firsts:
            for k in range(together):
                o_re, o_im = wave[k, 0], wave[k, 1]
                exits = []
                for m in range(first, first + group):
                    p_re, p_im = probe[0, m], probe[1, m]
                    exits.append(
                        jnp.concatenate([p_re * o_re - p_im * o_im, p_re * o_im + p_im * o_re], 1)
                    )
                halves[k, first] = times_table(jnp.concatenate(exits, 0), fwd_right)
        for first in firsts:
            for k in range(together):
                parts = [halves[k, first][j * pix : (j + 1) * pix] for j in range(group)]
                stacked = jnp.concatenate(
                    [jnp.concatenate([x[:, :pix], x[:, pix:]], 0) for x in parts], 1
                )
                full = table_times(inv_left, stacked)
                far[k, :, first * pix : (first + group) * pix] = full
                for j in range(group):
                    block = full[:, j * pix : (j + 1) * pix]
                    term = block[:pix] * block[:pix] + block[pix:] * block[pix:]
                    intensity[k] = term if intensity[k] is None else intensity[k] + term
        factors = []
        for k, p in enumerate(at):
            size = jnp.maximum(jnp.sqrt(intensity[k]) * (1.0 / pix), 0.5)
            factors.append(amp[p] / size * (1.0 / (pix * pix)))
        for first in firsts:
            for k in range(together):
                both = jnp.concatenate([factors[k]] * 2, 0)
                scaled = far[k, :, first * pix : (first + group) * pix]
                scaled = scaled * jnp.concatenate([both] * group, 1)
                halves[k, first] = table_times(fwd_left, scaled)
        change = [None] * together
        for first in firsts:
            grown = [None] * (2 * group)
            for k in range(together):
                o_re, o_im = wave[k, 0], wave[k, 1]
                parts = [halves[k, first][:, j * pix : (j + 1) * pix] for j in range(group)]
                flat = jnp.concatenate(
                    [jnp.concatenate([x[:pix], x[pix:]], 1) for x in parts], 0
                )
                back = times_table(flat, inv_right)
                if change[k] is None:
                    change[k] = [-power[...] * o_re, -power[...] * o_im]
                for j in range(group):
                    b_re = back[j * pix : (j + 1) * pix, :pix]
                    b_im = back[j * pix : (j + 1) * pix, pix:]
                    p_re, p_im = probe[0, first + j], probe[1, first + j]
                    change[k][0] += p_re * b_re + p_im * b_im
                    change[k][1] += p_re * b_im - p_im * b_re
                    for part, term in (
                        (2 * j, o_re * b_re + o_im * b_im),
                        (2 * j + 1, o_re * b_im - o_im * b_re),
                    ):
                        grown[part] = term if grown[part] is None else grown[part] + term
            for j in range(group):
                sums[first + j] += grown[2 * j]
                sums[modes + first + j] += grown[2 * j + 1]
        sums[2 * modes] += sum(
            wave[k, 0] * wave[k, 0] + wave[k, 1] * wave[k, 1] for k in range(together)
        )
        for k, (rows, lanes, shift, down) in enumerate(places):
            for plane in range(2):
                moved = jnp.concatenate([change[k][plane], jnp.zeros((8, pix), jnp.float32)], 0)
                moved = pltpu.roll(moved, down, 0)
                moved = jnp.concatenate([moved, jnp.zeros_like(moved)], 1)
                upd[plane, rows, lanes] += pltpu.roll(moved, shift, 1)
        return carry

    lax.fori_loop(0, (count[0, 0] + together - 1) // together, body, 0)


def run_pass(ext, probe, amp, starts, counts, tables, rows_padded):
    modes, pix = probe.shape[1], probe.shape[2]
    planes = rows_padded // pix
    return pl.pallas_call(
        pass_kernel,
        out_shape=(
            jax.ShapeDtypeStruct(ext.shape, jnp.float32),
            jax.ShapeDtypeStruct((planes, pix, pix), jnp.float32),
        ),
        in_specs=[SMEM, SMEM] + [VMEM] * 7,
        out_specs=(VMEM, VMEM),
        scratch_shapes=[
            pltpu.VMEM((pix, pix), jnp.float32),
            pltpu.VMEM((TOGETHER, 2 * pix, modes * pix), jnp.float32),
            pltpu.VMEM((TOGETHER, 2, pix, pix), jnp.float32),
        ],
        compiler_params=pltpu.CompilerParams(vmem_limit_bytes=LIMIT),
        name="scan_pass",
    )(starts, counts, ext, probe, amp, *tables)


def col_factors(n_row, n_col):
    core = math.gcd(2, n_col)
    far = math.gcd(4, n_col // core)
    return core, n_row * (n_col // core // far), far


def half_pack(re, im, upper):
    width = re.shape[-1]
    lane = lax.broadcasted_iota(jnp.int32, re.shape, 1)
    if upper:
        return jnp.where(lane < width // 2, pltpu.roll(re, width // 2, 1), im)
    return jnp.where(lane < width // 2, re, pltpu.roll(im, width // 2, 1))


def half_unpack(packed, upper):
    width = packed.shape[-1]
    lane = lax.broadcasted_iota(jnp.int32, packed.shape, 1)
    turned = pltpu.roll(packed, width // 2, 1)
    if upper:
        inside = lane >= width // 2
        return jnp.where(inside, turned, 0.0), jnp.where(inside, packed, 0.0)
    inside = lane < width // 2
    return jnp.where(inside, packed, 0.0), jnp.where(inside, turned, 0.0)


def exchange_kernel(kind, rim, modes, pix, *refs):
    reduce = kind != "rim"
    if reduce:
        (upd, ext, probe, sums, ext_out, probe_out) = refs[:6]
        scratch = refs[6:]
    else:
        (field, patterns, scales, ext_out, amp) = refs[:5]
        scratch = refs[5:]
    work, low_r, high_r, low_c, high_c, low_s, high_s, send_r, recv_r, send_c, recv_c = scratch[:11]
    full_rows, full_cols = work.shape[1], work.shape[2]
    wide = 2 * rim
    packed = kind != "all"
    if kind == "rim":
        send_high, send_low = (full_rows - wide, rim), (rim, rim)
        put_low, put_high = (0, rim), (full_rows - rim, rim)
    elif kind == "all":
        send_high, send_low = (full_rows - wide, wide), (0, wide)
        put_low, put_high = (0, wide), (full_rows - wide, wide)
    else:
        send_high, send_low = (full_rows - rim, rim), (0, rim)
        put_low, put_high = (rim, rim), (full_rows - wide, rim)
    put_middle = (sum(put_low), put_high[0] - sum(put_low))
    top = put_low[0]
    blocks = [put_low, put_middle, put_high]
    n_row, n_col = lax.axis_size("row"), lax.axis_size("col")
    me_row, me_col = lax.axis_index("row"), lax.axis_index("col")
    row_low, row_high = me_row > 0, me_row < n_row - 1
    col_low, col_high = me_col > 0, me_col < n_col - 1

    barrier = pltpu.get_barrier_semaphore()

    def greet(target):
        pl.semaphore_signal(barrier, inc=1, device_id=target, device_id_type=MESH)

    pl.when(row_low)(lambda: greet({"row": me_row - 1}))
    pl.when(row_high)(lambda: greet({"row": me_row + 1}))
    pl.when(col_low)(lambda: greet({"col": me_col - 1}))
    pl.when(col_high)(lambda: greet({"col": me_col + 1}))
    greeted = sum(x.astype(jnp.int32) for x in (row_low, row_high, col_low, col_high))
    stages = []
    if reduce:
        core, plane, far = col_factors(n_row, n_col)
        near = plane // n_row
        c = lax.rem(me_col, core)
        y = lax.rem(lax.div(me_col, core), near)
        z = lax.div(me_col, core * near)

        def in_core(q):
            return me_row, me_col + q - c

        def in_plane(q):
            return lax.div(q, near), me_col + (lax.rem(q, near) - y) * core

        def across(q):
            return me_row, me_col + (q - z) * (near * core)

        mine_plane, mine_far = me_row * near + y, z
        orders = [(plane, mine_plane, in_plane), (far, mine_far, across)]
        if plane == far and core == 2:
            def pick(first, second):
                return jnp.where(c == 0, first, second)

            def begin(q):
                return tuple(pick(a, b) for a, b in zip(in_plane(q), across(q)))

            def end(q):
                return tuple(pick(a, b) for a, b in zip(across(q), in_plane(q)))

            orders = [
                (far, pick(mine_plane, mine_far), begin),
                (far, pick(mine_far, mine_plane), end),
            ]
        for size, mine, where in [(core, c, in_core)] + orders:
            others = []
            for d in range(1, size):
                q = lax.rem(mine + d, size)
                row, col = where(q)
                others.append((q, {"row": row, "col": col}))
            if others:
                stages.append((size, mine, others))
        for _, _, others in stages:
            for _, target in others:
                greet(target)
        greeted = greeted + sum(len(stage[2]) for stage in stages)

    if reduce:
        border = upd
    else:
        border = work
        blank = jnp.zeros((field.shape[1], wide), jnp.float32)
        work[...] = jnp.zeros_like(work)
        for k in range(2):
            work[k, rim:-rim, :] = pltpu.roll(jnp.concatenate([field[k], blank], 1), rim, 1)
    pl.semaphore_wait(barrier, greeted)

    def copy_to(src, dst, send, recv, target):
        return pltpu.make_async_remote_copy(
            src_ref=src,
            dst_ref=dst,
            send_sem=send,
            recv_sem=recv,
            device_id=target,
            device_id_type=MESH,
        )

    row_up = copy_to(
        border.at[:, pl.ds(*send_high), :], low_r, send_r.at[0], recv_r.at[0], {"row": me_row + 1}
    )
    row_down = copy_to(
        border.at[:, pl.ds(*send_low), :], high_r, send_r.at[1], recv_r.at[1], {"row": me_row - 1}
    )
    pl.when(row_high)(row_up.start)
    pl.when(row_low)(row_down.start)

    col_up, col_down = [], []
    for index, (start, length) in enumerate(blocks):
        at = pl.ds(start - top, length)
        if packed:
            sources = high_s.at[at, :], low_s.at[at, :]
            places = low_c.at[at, :], high_c.at[at, :]
        else:
            span = pl.ds(start, length)
            sources = work.at[:, span, pl.ds(full_cols - wide, wide)], work.at[:, span, pl.ds(0, wide)]
            places = low_c.at[:, at, :], high_c.at[:, at, :]
        sems = send_c.at[0, index], recv_c.at[0, index]
        col_up.append(copy_to(sources[0], places[0], *sems, {"col": me_col + 1}))
        sems = send_c.at[1, index], recv_c.at[1, index]
        col_down.append(copy_to(sources[1], places[1], *sems, {"col": me_col - 1}))

    def start_block(index):
        start, length = blocks[index]
        if packed:
            span, at = pl.ds(start, length), pl.ds(start - top, length)
            high, low = pl.ds(full_cols - wide, wide), pl.ds(0, wide)
            upper = kind == "tile"
            high_s[at, :] = half_pack(work[0, span, high], work[1, span, high], upper)
            low_s[at, :] = half_pack(work[0, span, low], work[1, span, low], not upper)
        pl.when(col_high)(col_up[index].start)
        pl.when(col_low)(col_down[index].start)

    def begin_cols():
        if reduce:
            work[...] = upd[...]
        start_block(1)
        pl.when(jnp.logical_not(row_low))(lambda: start_block(0))
        pl.when(jnp.logical_not(row_high))(lambda: start_block(2))

    def finish_rows():
        @pl.when(row_low)
        def _():
            row_up.wait_recv()
            work[:, pl.ds(*put_low), :] += low_r[...]
            start_block(0)

        @pl.when(row_high)
        def _():
            row_down.wait_recv()
            work[:, pl.ds(*put_high), :] += high_r[...]
            start_block(2)

    def finish_cols():
        ext_out[...] = work[...]
        span = pl.ds(top, sum(put_high) - top)

        def land(copies, buffer, start, upper):
            for copy in copies:
                copy.wait_recv()
            lanes = pl.ds(start, wide)
            if packed:
                re, im = half_unpack(buffer[...], upper)
                ext_out[0, span, lanes] += re
                ext_out[1, span, lanes] += im
            else:
                ext_out[:, span, lanes] += buffer[...]

        pl.when(col_low)(lambda: land(col_up, low_c, 0, kind == "tile"))
        pl.when(col_high)(lambda: land(col_down, high_c, full_cols - wide, kind != "tile"))

    def drain():
        pl.when(row_high)(row_up.wait_send)
        pl.when(row_low)(row_down.wait_send)
        for index in range(3):
            pl.when(col_high)(col_up[index].wait_send)
            pl.when(col_low)(col_down[index].wait_send)

    if not reduce:
        begin_cols()
        for p in range(amp.shape[0]):
            column = jnp.broadcast_to(scales[p : p + 1, :], (pix, pix)).T
            amp[p] = patterns[p].astype(jnp.float32) * column
        finish_rows()
        finish_cols()
        drain()
        return

    acc, gat, send_s, recv_s, send_g, recv_g = scratch[11:17]
    landings = scratch[17:]
    pending = []
    offset, length, slot = 0, acc.shape[0], 0
    acc[...] = sums[...].reshape(acc.shape)
    spans = []
    for index, (size, mine, others) in enumerate(stages):
        piece = length // size
        spans.append((offset, piece, slot))
        copies = []
        for d, (q, target) in enumerate(others):
            copy = copy_to(
                acc.at[pl.ds(pl.multiple_of(offset + q * piece, 8), piece)],
                landings[index].at[d],
                send_s.at[slot],
                recv_s.at[slot],
                target,
            )
            slot += 1
            copy.start()
            copies.append(copy)
        if index == 0:
            begin_cols()
        keep = pl.ds(pl.multiple_of(offset + mine * piece, 8), piece)
        total = acc[keep, :]
        for d, copy in enumerate(copies):
            copy.wait_recv()
            total = total + landings[index][d]
        acc[keep, :] = total
        pending += copies
        offset, length = offset + mine * piece, piece

    keep = pl.ds(pl.multiple_of(offset, 8), length)
    gat[keep, :] = acc[keep, :]
    for index in reversed(range(len(stages))):
        size, mine, others = stages[index]
        start, piece, first = spans[index]
        own = pl.ds(pl.multiple_of(start + mine * piece, 8), piece)
        copies = []
        for d, (_, target) in enumerate(others):
            copy = copy_to(
                gat.at[own], gat.at[own], send_g.at[first + d], recv_g.at[first + d], target
            )
            copy.start()
            copies.append(copy)
        if index == len(stages) - 1:
            finish_rows()
        if index == 0:
            finish_cols()
            peak = jnp.max(jnp.sum(probe[0] * probe[0] + probe[1] * probe[1], axis=0))
            change = ext_out[...] / peak
            if kind == "all":
                rows_at = lax.broadcasted_iota(jnp.int32, (full_rows, full_cols), 0)
                cols_at = lax.broadcasted_iota(jnp.int32, (full_rows, full_cols), 1)
                first_row = jnp.where(me_row == 0, rim, 0)
                last_row = jnp.where(me_row == n_row - 1, full_rows - rim, full_rows)
                first_col = jnp.where(me_col == 0, rim, 0)
                last_col = jnp.where(me_col == n_col - 1, full_cols - rim, full_cols)
                inside = (rows_at >= first_row) & (rows_at < last_row)
                inside = inside & (cols_at >= first_col) & (cols_at < last_col)
                change = jnp.where(inside[None], change, 0.0)
            ext_out[...] = ext[...] + change
        for d in range(size - 1):
            sender = lax.rem(mine + size - 1 - d, size)
            place = gat.at[pl.ds(pl.multiple_of(start + sender * piece, 8), piece)]
            copy_to(place, place, send_g.at[first + d], recv_g.at[first + d], others[d][1]).wait_recv()
        pending += copies

    weight = gat[pl.ds(2 * modes * pix, pix), :]
    for k in range(2):
        for m in range(modes):
            probe_out[k, m] = gat[pl.ds((k * modes + m) * pix, pix), :] / weight
    for copy in pending:
        copy.wait_send()
    drain()


def exchange(kind, ident, shape, pix, operands):
    rim = pix // 2
    full_rows, full_cols = shape[1], shape[2]
    wide = 2 * rim
    row_width = wide if kind == "all" else rim
    height = full_rows - wide if kind == "tile" else full_rows
    n_row, n_col = lax.axis_size("row"), lax.axis_size("col")
    side = (2, height, wide) if kind == "all" else (height, wide)
    scratch = [
        pltpu.VMEM(shape, jnp.float32),
        pltpu.VMEM((2, row_width, full_cols), jnp.float32),
        pltpu.VMEM((2, row_width, full_cols), jnp.float32),
    ]
    scratch += [pltpu.VMEM(side, jnp.float32)] * 4
    scratch += [pltpu.SemaphoreType.DMA((2,))] * 2
    scratch += [pltpu.SemaphoreType.DMA((2, 3))] * 2
    out = jax.ShapeDtypeStruct(shape, jnp.float32)
    modes = 0
    if kind == "rim":
        outs = (out, jax.ShapeDtypeStruct(operands[1].shape, jnp.float32))
    else:
        probe, sums = operands[2:]
        modes = probe.shape[1]
        outs = (out, jax.ShapeDtypeStruct(probe.shape, jnp.float32))
        rows = sums.shape[0] * pix
        factors = [f for f in col_factors(n_row, n_col) if f > 1]
        hops = sum(f - 1 for f in factors)
        scratch += [pltpu.VMEM((rows, pix), jnp.float32)] * 2
        scratch += [pltpu.SemaphoreType.DMA((hops,))] * 4
        length = rows
        for f in factors:
            length //= f
            scratch.append(pltpu.VMEM((f - 1, length, pix), jnp.float32))
    return pl.pallas_call(
        functools.partial(exchange_kernel, kind, rim, modes, pix),
        out_shape=outs,
        in_specs=[VMEM] * len(operands),
        out_specs=tuple([VMEM] * len(outs)),
        scratch_shapes=scratch,
        compiler_params=pltpu.CompilerParams(
            collective_id=ident, has_side_effects=True, vmem_limit_bytes=LIMIT
        ),
        name="exchange_" + kind,
    )(*operands)


def on_device(object_field, probe, patterns, row_scales, positions, counts):
    modes, pix = probe.shape[1], probe.shape[2]
    rim = pix // 2
    tables = [jnp.asarray(t) for t in dft_tables(pix)]
    starts = positions[0, 0]
    step = math.lcm(8 * lax.axis_size("row") * lax.axis_size("col"), pix)
    rows_padded = -(-(2 * modes + 1) * pix // step) * step
    shape = (2, object_field.shape[1] + pix, object_field.shape[2] + pix)
    ext, amp = exchange("rim", 0, shape, pix, (object_field, patterns[0, 0], row_scales[0, 0]))
    for pass_number in range(PASSES):
        upd, sums = run_pass(ext, probe, amp, starts, counts, tables, rows_padded)
        kind = "tile" if pass_number == PASSES - 1 else "all"
        ext, probe = exchange(kind, pass_number + 1, shape, pix, (upd, ext, probe, sums))
    return (ext[:, rim:-rim, rim:-rim], probe)


def solution(mesh):
    placed = (
        P(None, "row", "col"),
        P(),
        P("row", "col", None, None, None),
        P("row", "col", None, None),
        P("row", "col", None, None),
        P("row", "col"),
    )
    return jax.shard_map(
        on_device,
        mesh=mesh,
        in_specs=placed,
        out_specs=(P(None, "row", "col"), P()),
        check_vma=False,
    )
```

profile of v0, /device:TPU:0, one launch (start us, length us, event | category | flops | bytes accessed | tf_op | source)
XLA Modules:
  0.0 101.3 jit_solution(12120392620224891558)
XLA Ops:
  1.3 0.8 copy.13.pos
  2.0 1.0 %copy-done.10 = f32[2,256,256]{2,1,0:T(8,128)S(1)} copy-done((f32[2,256,256]{2,1,0:T(8,128)S(1)}, f32[2,256,256]{2,1,0:T(8,128)}, u32[]{:S(2)}) %copy-start.10) | copy-done | bytes 524312
  3.1 0.9 copy-done.11
  4.0 0.7 copy-done.12
  4.7 9.8 %exchange_rim.1 = (f32[2,384,384]{2,1,0:T(8,128)S(1)}, f32[8,128,128]{2,1,0:T(8,128)S(1)}) custom-call(f32[2,256,256]{2,1,0:T(8,128)S(1)} %copy-done.10, bf16[8,128,128]{2,1,0:T(8,128)(2,1)S(1)} %bitcast.3, f32[8,128]{1,0:T(8,128)S(1)} %bitcast.4), custom_call_target="tpu_custom_call" | custom-call | tf_op jit(solution)/shard_map/exchange_rim/pallas_call | solution.py:500
  14.5 0.0 copy-start
  14.5 1.0 %copy-done = f32[2,4,128,128]{3,2,1,0:T(8,128)S(1)} copy-done((f32[2,4,128,128]{3,2,1,0:T(8,128)S(1)}, f32[2,4,128,128]{3,2,1,0:T(8,128)}, u32[]{:S(2)}) %copy-start) | copy-done | bytes 524312
  15.5 1.0 copy-done.2
  16.5 1.0 copy-done.4
  17.5 1.0 copy-done.6
  18.5 1.0 copy-done.8
  19.5 11.5 %scan_pass.2 = (f32[2,384,384]{2,1,0:T(8,128)S(1)}, f32[10,128,128]{2,1,0:T(8,128)S(1)}) custom-call(s32[8,2]{1,0:T(8,128)S(1)} %copy.13.pos, s32[1,1]{1,0:T(1,128)S(6)} %copy.15.count, f32[2,384,384]{2,1,0:T(8,128)S(1)} %get-tuple-element.12.ext.refs_1_, f32[2,4,128,128]{3,2,1,0:T(8,128)S(1)} %copy-done, f32[8,128,128]{2,1,0:T(8,128)S(1)} %get-tuple-element.13.amp, ...), custom_call_target="tpu_custom_call" | custom-call | tf_op jit(solution)/shard_map/scan_pass/pallas_call | solution.py:152
  31.1 0.0 copy-start.3
  31.1 0.0 copy-start.5
  31.1 0.0 copy-start.7
  31.1 0.0 copy-start.9
  31.1 32.0 %exchange_all.1 = (f32[2,384,384]{2,1,0:T(8,128)S(1)}, f32[2,4,128,128]{3,2,1,0:T(8,128)S(1)}) custom-call(f32[2,384,384]{2,1,0:T(8,128)S(1)} %get-tuple-element.14.refs_0_, f32[2,384,384]{2,1,0:T(8,128)S(1)} %get-tuple-element.12.ext.refs_1_, f32[2,4,128,128]{3,2,1,0:T(8,128)S(1)} %copy-done.1, f32[10,128,128]{2,1,0:T(8,128)S(1)} %get-tuple-element.15.refs_3_), custom_call_target="tpu_custom_call" | custom-call | tf_op jit(solution)/shard_map/exchange_all/pallas_call | solution.py:500
  63.1 0.0 copy-done.3
  63.1 0.0 copy-done.5
  63.1 0.0 copy-done.7
  63.2 11.5 %scan_pass.3 = (f32[2,384,384]{2,1,0:T(8,128)S(1)}, f32[10,128,128]{2,1,0:T(8,128)S(1)}) custom-call(s32[8,2]{1,0:T(8,128)S(1)} %copy.13.pos, s32[1,1]{1,0:T(1,128)S(6)} %copy.15.count, f32[2,384,384]{2,1,0:T(8,128)S(1)} %get-tuple-element.16.ext.refs_1_, f32[2,4,128,128]{3,2,1,0:T(8,128)S(1)} %get-tuple-element.17.probe.refs_2_, ...), custom_call_target="tpu_custom_call" | custom-call | tf_op jit(solution)/shard_map/scan_pass/pallas_call | solution.py:152
  74.7 24.9 %exchange_tile.1 = (f32[2,384,384]{2,1,0:T(8,128)S(1)}, f32[2,4,128,128]{3,2,1,0:T(8,128)S(1)}) custom-call(f32[2,384,384]{2,1,0:T(8,128)S(1)} %get-tuple-element.18.refs_0_, f32[2,384,384]{2,1,0:T(8,128)S(1)} %get-tuple-element.16.ext.refs_1_, f32[2,4,128,128]{3,2,1,0:T(8,128)S(1)} %get-tuple-element.17.probe.refs_2_, ...), custom_call_target="tpu_custom_call" | custom-call | tf_op jit(solution)/shard_map/exchange_tile/pallas_call | solution.py:500
  99.6 1.0 slice.3
  100.6 0.8 copy.16
  (10 shorter events, 0.0 us)
Async XLA Ops:
  2.0 1.0 %copy-start.10 = (f32[2,256,256]{2,1,0:T(8,128)S(1)}, f32[2,256,256]{2,1,0:T(8,128)}, u32[]{:S(2)}) copy-start(f32[2,256,256]{2,1,0:T(8,128)} %refs_0_.1) | copy-start | bytes 1572868
  3.1 0.9 copy-start.11
  4.0 0.7 copy-start.12
  14.5 1.0 %copy-start = (f32[2,4,128,128]{3,2,1,0:T(8,128)S(1)}, f32[2,4,128,128]{3,2,1,0:T(8,128)}, u32[]{:S(2)}) copy-start(f32[2,4,128,128]{3,2,1,0:T(8,128)} %refs_2_.1) | copy-start | bytes 1572868
  15.5 1.0 copy-start.2
  16.5 1.0 copy-start.4
  17.5 1.0 copy-start.6
  18.5 1.0 copy-start.8
  19.5 11.5 %copy-start.1 = (f32[2,4,128,128]{3,2,1,0:T(8,128)S(1)}, f32[2,4,128,128]{3,2,1,0:T(8,128)}, u32[]{:S(2)}) copy-start(f32[2,4,128,128]{3,2,1,0:T(8,128)} %refs_2_.1) | copy-start | bytes 1572868
  31.1 32.1 %copy-start.3 = (bf16[256,768]{1,0:T(8,128)(2,1)S(1)}, bf16[256,768]{1,0:T(8,128)(2,1)}, u32[]{:S(2)}) copy-start(bf16[256,768]{1,0:T(8,128)(2,1)} %constant.11.clone.inv_left) | copy-start | bytes 1179652
  31.1 32.1 %copy-start.5 = (bf16[256,768]{1,0:T(8,128)(2,1)S(1)}, bf16[256,768]{1,0:T(8,128)(2,1)}, u32[]{:S(2)}) copy-start(bf16[256,768]{1,0:T(8,128)(2,1)} %constant.10.clone.fwd_left) | copy-start | bytes 1179652
  31.1 32.1 %copy-start.7 = (bf16[768,256]{1,0:T(8,128)(2,1)S(1)}, bf16[768,256]{1,0:T(8,128)(2,1)}, u32[]{:S(2)}) copy-start(bf16[768,256]{1,0:T(8,128)(2,1)} %constant.9.clone.inv_right) | copy-start | bytes 1179652
  31.1 32.1 %copy-start.9 = (bf16[768,256]{1,0:T(8,128)(2,1)S(1)}, bf16[768,256]{1,0:T(8,128)(2,1)}, u32[]{:S(2)}) copy-start(bf16[768,256]{1,0:T(8,128)(2,1)} %constant.8.clone.fwd_right) | copy-start | bytes 1179652
where the time goes:
time: 102 us; the launch traced here: 101 us
  Pallas kernels  89.7 us (88%)
  local copies, waits for them, and re-layouts  10.3 us (10%)
  between operations  1.4 us (1%)
    pallas_call x3, Pallas kernels, exchange(): pl.pallas_call(functools.partial(exchange_kernel, kind, rim, modes, pix),...  66.7 us
    pallas_call x2, Pallas kernels, run_pass(): pl.pallas_call(pass_kernel, out_shape=(jax.ShapeDtypeStruct(ext.shape, jn...  23 us
    unnamed x27, local copies, waits for them, and re-layouts  8.52 us

commit v1 on v0

--- a/solution.py
+++ b/solution.py
@@ -13,6 +13,7 @@
 TOGETHER = 2
 MESH = pl.DeviceIdType.MESH
 VMEM = pl.BlockSpec(memory_space=pltpu.VMEM)
+HBM = pl.BlockSpec(memory_space=pltpu.HBM)
 SMEM = pl.BlockSpec(memory_space=pltpu.SMEM)
 LIMIT = 48 * 1024 * 1024
 
@@ -23,13 +24,11 @@
     cosine, sine = np.cos(angle), np.sin(angle)
     forward = np.block([[cosine, -sine], [sine, cosine]]).astype(np.float32)
     inverse = np.block([[cosine, sine], [-sine, cosine]]).astype(np.float32)
-    rights, lefts = [], []
+    out = []
     for table in (forward, inverse):
         high = table.astype(jnp.bfloat16)
-        low = (table - high.astype(np.float32)).astype(jnp.bfloat16)
-        rights.append(np.concatenate([high, high, low], 0))
-        lefts.append(np.concatenate([high, high, low], 1))
-    return rights + lefts
+        out.append(np.stack([high, (table - high.astype(np.float32)).astype(jnp.bfloat16)]))
+    return np.stack(out)
 
 
 def split(value, axis):
@@ -39,16 +38,21 @@
 
 
 def times_table(value, table):
-    return jnp.dot(split(value, 1), table[...], preferred_element_type=jnp.float32)
+    high, low = table[0], table[1]
+    joined = jnp.concatenate([high, high, low], 0)
+    return jnp.dot(split(value, 1), joined, preferred_element_type=jnp.float32)
 
 
 def table_times(table, value):
-    return jnp.dot(table[...], split(value, 0), preferred_element_type=jnp.float32)
+    high, low = table[0], table[1]
+    joined = jnp.concatenate([high, high, low], 1)
+    return jnp.dot(joined, split(value, 0), preferred_element_type=jnp.float32)
 
 
 def pass_kernel(
-    pos, count, ext, probe, amp, fwd_right, inv_right, fwd_left, inv_left, upd, sums, power, far, wave
+    pos, count, ext, probe, amp, table, upd, sums, power, far, wave
 ):
+    forward, inverse = table.at[0], table.at[1]
     modes, pix = probe.shape[1], probe.shape[2]
     group = 2 if modes % 2 == 0 else 1
     firsts = range(0, modes, group)
@@ -83,14 +87,14 @@
                     exits.append(
                         jnp.concatenate([p_re * o_re - p_im * o_im, p_re * o_im + p_im * o_re], 1)
                     )
-                halves[k, first] = times_table(jnp.concatenate(exits, 0), fwd_right)
+                halves[k, first] = times_table(jnp.concatenate(exits, 0), forward)
         for first in firsts:
             for k in range(together):
                 parts = [halves[k, first][j * pix : (j + 1) * pix] for j in range(group)]
                 stacked = jnp.concatenate(
                     [jnp.concatenate([x[:, :pix], x[:, pix:]], 0) for x in parts], 1
                 )
-                full = table_times(inv_left, stacked)
+                full = table_times(inverse, stacked)
                 far[k, :, first * pix : (first + group) * pix] = full
                 for j in range(group):
                     block = full[:, j * pix : (j + 1) * pix]
@@ -105,7 +109,7 @@
                 both = jnp.concatenate([factors[k]] * 2, 0)
                 scaled = far[k, :, first * pix : (first + group) * pix]
                 scaled = scaled * jnp.concatenate([both] * group, 1)
-                halves[k, first] = table_times(fwd_left, scaled)
+                halves[k, first] = table_times(forward, scaled)
         change = [None] * together
         for first in firsts:
             grown = [None] * (2 * group)
@@ -115,7 +119,7 @@
                 flat = jnp.concatenate(
                     [jnp.concatenate([x[:pix], x[pix:]], 1) for x in parts], 0
                 )
-                back = times_table(flat, inv_right)
+                back = times_table(flat, inverse)
                 if change[k] is None:
                     change[k] = [-power[...] * o_re, -power[...] * o_im]
                 for j in range(group):
@@ -146,7 +150,7 @@
     lax.fori_loop(0, (count[0, 0] + together - 1) // together, body, 0)
 
 
-def run_pass(ext, probe, amp, starts, counts, tables, rows_padded):
+def run_pass(ext, probe, amp, starts, counts, table, rows_padded):
     modes, pix = probe.shape[1], probe.shape[2]
     planes = rows_padded // pix
     return pl.pallas_call(
@@ -155,7 +159,7 @@
             jax.ShapeDtypeStruct(ext.shape, jnp.float32),
             jax.ShapeDtypeStruct((planes, pix, pix), jnp.float32),
         ),
-        in_specs=[SMEM, SMEM] + [VMEM] * 7,
+        in_specs=[SMEM, SMEM] + [VMEM] * 4,
         out_specs=(VMEM, VMEM),
         scratch_shapes=[
             pltpu.VMEM((pix, pix), jnp.float32),
@@ -164,7 +168,7 @@
         ],
         compiler_params=pltpu.CompilerParams(vmem_limit_bytes=LIMIT),
         name="scan_pass",
-    )(starts, counts, ext, probe, amp, *tables)
+    )(starts, counts, ext, probe, amp, table)
 
 
 def col_factors(n_row, n_col):
@@ -192,14 +196,33 @@
     return jnp.where(inside, packed, 0.0), jnp.where(inside, turned, 0.0)
 
 
+def partners(stage):
+    size, mine, where = stage
+    found = []
+    for d in range(1, size):
+        q = lax.rem(mine + d, size)
+        row, col = where(q)
+        found.append((q, {"row": row, "col": col}))
+    return found
+
+
 def exchange_kernel(kind, rim, modes, pix, *refs):
     reduce = kind != "rim"
     if reduce:
         (upd, ext, probe, sums, ext_out, probe_out) = refs[:6]
         scratch = refs[6:]
     else:
-        (field, patterns, scales, ext_out, amp) = refs[:5]
-        scratch = refs[5:]
+        (field_in, patterns_in, scales_in, table, probe, ext_out, amp, table_out, probe_out) = refs[:9]
+        scratch = refs[9:]
+        field, patterns, scales, local = scratch[11:]
+        field_copy = pltpu.make_async_copy(field_in, field, local.at[0])
+        pattern_copy = pltpu.make_async_copy(patterns_in, patterns, local.at[1])
+        scale_copy = pltpu.make_async_copy(scales_in, scales, local.at[2])
+        keep_table = pltpu.make_async_copy(table, table_out, local.at[3])
+        keep_probe = pltpu.make_async_copy(probe, probe_out, local.at[4])
+        field_copy.start()
+        pattern_copy.start()
+        scale_copy.start()
     work, low_r, high_r, low_c, high_c, low_s, high_s, send_r, recv_r, send_c, recv_c = scratch[:11]
     full_rows, full_cols = work.shape[1], work.shape[2]
     wide = 2 * rim
@@ -231,7 +254,7 @@
     pl.when(col_low)(lambda: greet({"col": me_col - 1}))
     pl.when(col_high)(lambda: greet({"col": me_col + 1}))
     greeted = sum(x.astype(jnp.int32) for x in (row_low, row_high, col_low, col_high))
-    stages = []
+    chunks = []
     if reduce:
         core, plane, far = col_factors(n_row, n_col)
         near = plane // n_row
@@ -248,34 +271,15 @@
         def across(q):
             return me_row, me_col + (q - z) * (near * core)
 
-        mine_plane, mine_far = me_row * near + y, z
-        orders = [(plane, mine_plane, in_plane), (far, mine_far, across)]
-        if plane == far and core == 2:
-            def pick(first, second):
-                return jnp.where(c == 0, first, second)
-
-            def begin(q):
-                return tuple(pick(a, b) for a, b in zip(in_plane(q), across(q)))
-
-            def end(q):
-                return tuple(pick(a, b) for a, b in zip(across(q), in_plane(q)))
-
-            orders = [
-                (far, pick(mine_plane, mine_far), begin),
-                (far, pick(mine_far, mine_plane), end),
-            ]
-        for size, mine, where in [(core, c, in_core)] + orders:
-            others = []
-            for d in range(1, size):
-                q = lax.rem(mine + d, size)
-                row, col = where(q)
-                others.append((q, {"row": row, "col": col}))
-            if others:
-                stages.append((size, mine, others))
-        for _, _, others in stages:
-            for _, target in others:
+        in_chip = (core, c, in_core)
+        planar = (plane, me_row * near + y, in_plane)
+        distant = (far, z, across)
+        for order in ((in_chip, planar, distant), (in_chip, distant, planar)):
+            chunks.append([stage for stage in order if stage[0] > 1])
+        for stage in chunks[0]:
+            for _, target in partners(stage):
                 greet(target)
-        greeted = greeted + sum(len(stage[2]) for stage in stages)
+        greeted = greeted + sum(stage[0] - 1 for stage in chunks[0])
 
     if reduce:
         border = upd
@@ -283,6 +287,7 @@
         border = work
         blank = jnp.zeros((field.shape[1], wide), jnp.float32)
         work[...] = jnp.zeros_like(work)
+        field_copy.wait()
         for k in range(2):
             work[k, rim:-rim, :] = pltpu.roll(jnp.concatenate([field[k], blank], 1), rim, 1)
     pl.semaphore_wait(barrier, greeted)
@@ -303,8 +308,10 @@
     row_down = copy_to(
         border.at[:, pl.ds(*send_low), :], high_r, send_r.at[1], recv_r.at[1], {"row": me_row - 1}
     )
-    pl.when(row_high)(row_up.start)
-    pl.when(row_low)(row_down.start)
+
+    def start_rows():
+        pl.when(row_high)(row_up.start)
+        pl.when(row_low)(row_down.start)
 
     col_up, col_down = [], []
     for index, (start, length) in enumerate(blocks):
@@ -378,82 +385,123 @@
             pl.when(col_low)(col_down[index].wait_send)
 
     if not reduce:
+        start_rows()
         begin_cols()
+        keep_table.start()
+        keep_probe.start()
+        pattern_copy.wait()
+        scale_copy.wait()
         for p in range(amp.shape[0]):
             column = jnp.broadcast_to(scales[p : p + 1, :], (pix, pix)).T
             amp[p] = patterns[p].astype(jnp.float32) * column
         finish_rows()
         finish_cols()
+        keep_table.wait()
+        keep_probe.wait()
         drain()
         return
 
     acc, gat, send_s, recv_s, send_g, recv_g = scratch[11:17]
     landings = scratch[17:]
     pending = []
-    offset, length, slot = 0, acc.shape[0], 0
     acc[...] = sums[...].reshape(acc.shape)
-    spans = []
-    for index, (size, mine, others) in enumerate(stages):
-        piece = length // size
-        spans.append((offset, piece, slot))
+    half = acc.shape[0] // 2
+    states = []
+    for index, stages in enumerate(chunks):
+        spans, offset, length, slot = [], index * half, half, 0
+        for size, mine, _ in stages[:-1]:
+            length //= size
+            spans.append((offset, length, slot))
+            offset, slot = offset + mine * length, slot + size - 1
+        spans.append((offset, length, slot))
+        states.append((stages, spans, landings[index * len(stages) : (index + 1) * len(stages)]))
+
+    def rows_of(start, piece):
+        return pl.ds(pl.multiple_of(start, 8), piece)
+
+    def begin(index, step):
+        stages, spans, lands = states[index]
+        back = step >= len(stages)
+        at = 2 * len(stages) - 2 - step if back else step
+        stage = stages[at]
+        size, mine, _ = stage
+        start, piece, slot = spans[at]
+        own = rows_of(start + mine * piece, piece)
         copies = []
-        for d, (q, target) in enumerate(others):
-            copy = copy_to(
-                acc.at[pl.ds(pl.multiple_of(offset + q * piece, 8), piece)],
-                landings[index].at[d],
-                send_s.at[slot],
-                recv_s.at[slot],
-                target,
-            )
-            slot += 1
-            copy.start()
-            copies.append(copy)
-        if index == 0:
+        for d, (q, target) in enumerate(partners(stage)):
+            sems = send_s.at[index, slot + d], recv_s.at[index, slot + d]
+            if back:
+                sems = send_g.at[index, slot + d], recv_g.at[index, slot + d]
+                src, dst = gat.at[own], gat.at[own]
+            elif at == len(stages) - 1:
+                src, dst = acc.at[rows_of(start, piece)], lands[at].at[mine]
+            else:
+                src, dst = acc.at[rows_of(start + q * piece, piece)], lands[at].at[d]
+            copies.append(copy_to(src, dst, *sems, target))
+            copies[-1].start()
+        pending.extend(copies)
+        return copies
+
+    def end(index, step, copies):
+        stages, spans, lands = states[index]
+        back = step >= len(stages)
+        at = 2 * len(stages) - 2 - step if back else step
+        stage = stages[at]
+        size, mine, _ = stage
+        start, piece, slot = spans[at]
+        if not back and at < len(stages) - 1:
+            keep = rows_of(start + mine * piece, piece)
+            total = acc[keep, :]
+            for d, copy in enumerate(copies):
+                copy.wait_recv()
+                total = total + lands[at][d]
+            acc[keep, :] = total
+            return
+        if not back:
+            lands[at][mine] = acc[rows_of(start, piece), :]
+        for d, (_, target) in enumerate(partners(stage)):
+            sender = lax.rem(mine + size - 1 - d, size)
+            if back:
+                place = gat.at[rows_of(start + sender * piece, piece)]
+                sems = send_g.at[index, slot + d], recv_g.at[index, slot + d]
+            else:
+                place = lands[at].at[sender]
+                sems = send_s.at[index, slot + d], recv_s.at[index, slot + d]
+            copy_to(place, place, *sems, target).wait_recv()
+        if not back:
+            total = lands[at][0]
+            for q in range(1, size):
+                total = total + lands[at][q]
+            gat[rows_of(start, piece), :] = total
+
+    steps = 2 * len(chunks[0]) - 1
+    flying = [None, None]
+    for step in range(steps):
+        for index in range(2):
+            if step > 0:
+                end(index, step - 1, flying[index])
+            flying[index] = begin(index, step)
+        if step == (0 if kind == "all" else min(1, steps - 1)):
+            start_rows()
             begin_cols()
-        keep = pl.ds(pl.multiple_of(offset + mine * piece, 8), piece)
-        total = acc[keep, :]
-        for d, copy in enumerate(copies):
-            copy.wait_recv()
-            total = total + landings[index][d]
-        acc[keep, :] = total
-        pending += copies
-        offset, length = offset + mine * piece, piece
-
-    keep = pl.ds(pl.multiple_of(offset, 8), length)
-    gat[keep, :] = acc[keep, :]
-    for index in reversed(range(len(stages))):
-        size, mine, others = stages[index]
-        start, piece, first = spans[index]
-        own = pl.ds(pl.multiple_of(start + mine * piece, 8), piece)
-        copies = []
-        for d, (_, target) in enumerate(others):
-            copy = copy_to(
-                gat.at[own], gat.at[own], send_g.at[first + d], recv_g.at[first + d], target
-            )
-            copy.start()
-            copies.append(copy)
-        if index == len(stages) - 1:
+        if step == max(steps - 2, 0):
             finish_rows()
-        if index == 0:
-            finish_cols()
-            peak = jnp.max(jnp.sum(probe[0] * probe[0] + probe[1] * probe[1], axis=0))
-            change = ext_out[...] / peak
-            if kind == "all":
-                rows_at = lax.broadcasted_iota(jnp.int32, (full_rows, full_cols), 0)
-                cols_at = lax.broadcasted_iota(jnp.int32, (full_rows, full_cols), 1)
-                first_row = jnp.where(me_row == 0, rim, 0)
-                last_row = jnp.where(me_row == n_row - 1, full_rows - rim, full_rows)
-                first_col = jnp.where(me_col == 0, rim, 0)
-                last_col = jnp.where(me_col == n_col - 1, full_cols - rim, full_cols)
-                inside = (rows_at >= first_row) & (rows_at < last_row)
-                inside = inside & (cols_at >= first_col) & (cols_at < last_col)
-                change = jnp.where(inside[None], change, 0.0)
-            ext_out[...] = ext[...] + change
-        for d in range(size - 1):
-            sender = lax.rem(mine + size - 1 - d, size)
-            place = gat.at[pl.ds(pl.multiple_of(start + sender * piece, 8), piece)]
-            copy_to(place, place, send_g.at[first + d], recv_g.at[first + d], others[d][1]).wait_recv()
-        pending += copies
+    finish_cols()
+    peak = jnp.max(jnp.sum(probe[0] * probe[0] + probe[1] * probe[1], axis=0))
+    change = ext_out[...] / peak
+    if kind == "all":
+        rows_at = lax.broadcasted_iota(jnp.int32, (full_rows, full_cols), 0)
+        cols_at = lax.broadcasted_iota(jnp.int32, (full_rows, full_cols), 1)
+        first_row = jnp.where(me_row == 0, rim, 0)
+        last_row = jnp.where(me_row == n_row - 1, full_rows - rim, full_rows)
+        first_col = jnp.where(me_col == 0, rim, 0)
+        last_col = jnp.where(me_col == n_col - 1, full_cols - rim, full_cols)
+        inside = (rows_at >= first_row) & (rows_at < last_row)
+        inside = inside & (cols_at >= first_col) & (cols_at < last_col)
+        change = jnp.where(inside[None], change, 0.0)
+    ext_out[...] = ext[...] + change
+    for index in range(2):
+        end(index, steps - 1, flying[index])
 
     weight = gat[pl.ds(2 * modes * pix, pix), :]
     for k in range(2):
@@ -483,24 +531,35 @@
     out = jax.ShapeDtypeStruct(shape, jnp.float32)
     modes = 0
     if kind == "rim":
-        outs = (out, jax.ShapeDtypeStruct(operands[1].shape, jnp.float32))
+        field, patterns, scales, table, probe = operands
+        outs = (
+            out,
+            jax.ShapeDtypeStruct(patterns.shape, jnp.float32),
+            jax.ShapeDtypeStruct(table.shape, table.dtype),
+            jax.ShapeDtypeStruct(probe.shape, jnp.float32),
+        )
+        scratch += [pltpu.VMEM(x.shape, x.dtype) for x in (field, patterns, scales)]
+        scratch.append(pltpu.SemaphoreType.DMA((5,)))
     else:
         probe, sums = operands[2:]
         modes = probe.shape[1]
         outs = (out, jax.ShapeDtypeStruct(probe.shape, jnp.float32))
         rows = sums.shape[0] * pix
-        factors = [f for f in col_factors(n_row, n_col) if f > 1]
-        hops = sum(f - 1 for f in factors)
+        core, plane, far = col_factors(n_row, n_col)
+        hops = core + plane + far - 3
         scratch += [pltpu.VMEM((rows, pix), jnp.float32)] * 2
-        scratch += [pltpu.SemaphoreType.DMA((hops,))] * 4
-        length = rows
-        for f in factors:
-            length //= f
-            scratch.append(pltpu.VMEM((f - 1, length, pix), jnp.float32))
+        scratch += [pltpu.SemaphoreType.DMA((2, hops))] * 4
+        for order in ((core, plane, far), (core, far, plane)):
+            sizes = [f for f in order if f > 1]
+            length = rows // 2
+            for size in sizes[:-1]:
+                length //= size
+                scratch.append(pltpu.VMEM((size - 1, length, pix), jnp.float32))
+            scratch.append(pltpu.VMEM((sizes[-1], length, pix), jnp.float32))
     return pl.pallas_call(
         functools.partial(exchange_kernel, kind, rim, modes, pix),
         out_shape=outs,
-        in_specs=[VMEM] * len(operands),
+        in_specs=[HBM if kind == "rim" else VMEM] * len(operands),
         out_specs=tuple([VMEM] * len(outs)),
         scratch_shapes=scratch,
         compiler_params=pltpu.CompilerParams(
@@ -513,14 +572,17 @@
 def on_device(object_field, probe, patterns, row_scales, positions, counts):
     modes, pix = probe.shape[1], probe.shape[2]
     rim = pix // 2
-    tables = [jnp.asarray(t) for t in dft_tables(pix)]
+    table = jnp.asarray(dft_tables(pix))
     starts = positions[0, 0]
-    step = math.lcm(8 * lax.axis_size("row") * lax.axis_size("col"), pix)
+    core, plane, far = col_factors(lax.axis_size("row"), lax.axis_size("col"))
+    step = math.lcm(16 * core * max(plane, far), pix)
     rows_padded = -(-(2 * modes + 1) * pix // step) * step
     shape = (2, object_field.shape[1] + pix, object_field.shape[2] + pix)
-    ext, amp = exchange("rim", 0, shape, pix, (object_field, patterns[0, 0], row_scales[0, 0]))
+    ext, amp, table, probe = exchange(
+        "rim", 0, shape, pix, (object_field, patterns[0, 0], row_scales[0, 0], table, probe)
+    )
     for pass_number in range(PASSES):
-        upd, sums = run_pass(ext, probe, amp, starts, counts, tables, rows_padded)
+        upd, sums = run_pass(ext, probe, amp, starts, counts, table, rows_padded)
         kind = "tile" if pass_number == PASSES - 1 else "all"
         ext, probe = exchange(kind, pass_number + 1, shape, pix, (upd, ext, probe, sums))
     return (ext[:, rim:-rim, rim:-rim], probe)

time: 102 us -> 87.6 us (0.86)
  Pallas kernels: 89.7 us -> 78.8 us
  local copies, waits for them, and re-layouts: 10.3 us -> 7.3 us
    pallas_call x2, Pallas kernels: 23 us -> 16.9 us  [run_pass(): pl.pallas_call(pass_kernel, out_shape=(jax.ShapeDtypeStruct(ext.shape, jn...]
    pallas_call x3, Pallas kernels: 66.7 us -> 61.9 us  [exchange(): pl.pallas_call(functools.partial(exchange_kernel, kind, rim, modes, pix),...]
    unnamed x27 -> x11, local copies, waits for them, and re-layouts: 8.52 us -> 5.55 us
where the time goes in v1:
time: 87.6 us; the launch traced here: 87.4 us
  Pallas kernels  78.8 us (90%)
  local copies, waits for them, and re-layouts  7.3 us (8%)
  between operations  1.32 us (2%)
    pallas_call x3, Pallas kernels, exchange(): pl.pallas_call(functools.partial(exchange_kernel, kind, rim, modes, pix),...  61.9 us
    pallas_call x2, Pallas kernels, run_pass(): pl.pallas_call(pass_kernel, out_shape=(jax.ShapeDtypeStruct(ext.shape, jn...  16.9 us
    unnamed x11, local copies, waits for them, and re-layouts  5.55 us

profile of v1, /device:TPU:0, one launch (start us, length us, event | category | flops | bytes accessed | tf_op | source)
XLA Modules:
  0.0 87.4 jit_solution(200199165546794310)
XLA Ops:
  1.3 0.8 copy.10.pos
  2.0 0.0 copy-start
  2.0 1.0 %copy-done = f32[2,256,256]{2,1,0:T(8,128)S(1)} copy-done((f32[2,256,256]{2,1,0:T(8,128)S(1)}, f32[2,256,256]{2,1,0:T(8,128)}, u32[]{:S(2)}) %copy-start) | copy-done | bytes 524312
  3.1 0.0 copy-start.1
  3.1 1.0 %copy-done.1 = f32[2,4,128,128]{3,2,1,0:T(8,128)S(1)} copy-done((f32[2,4,128,128]{3,2,1,0:T(8,128)S(1)}, f32[2,4,128,128]{3,2,1,0:T(8,128)}, u32[]{:S(2)}) %copy-start.1) | copy-done | bytes 524312
  4.1 0.0 copy-start.2
  4.1 1.0 %copy-done.2 = bf16[2,2,256,256]{3,2,1,0:T(8,128)(2,1)S(1)} copy-done((bf16[2,2,256,256]{3,2,1,0:T(8,128)(2,1)S(1)}, bf16[2,2,256,256]{3,2,1,0:T(8,128)(2,1)}, u32[]{:S(2)}) %copy-start.2) | copy-done | bytes 524312
  5.2 0.0 copy-start.3
  5.2 0.9 %copy-done.3 = bf16[1,1,8,128,128]{4,3,2,1,0:T(8,128)(2,1)S(1)} copy-done((bf16[1,1,8,128,128]{4,3,2,1,0:T(8,128)(2,1)S(1)}, bf16[1,1,8,128,128]{4,3,2,1,0:T(8,128)(2,1)}, u32[]{:S(2)}) %copy-start.3) | copy-done | bytes 262168
  6.1 0.0 copy-start.4
  6.1 0.7 copy-done.4
  6.8 10.0 %exchange_rim.1 = (f32[2,384,384]{2,1,0:T(8,128)S(1)}, f32[8,128,128]{2,1,0:T(8,128)S(1)}, bf16[2,2,256,256]{3,2,1,0:T(8,128)(2,1)S(1)}, f32[2,4,128,128]{3,2,1,0:T(8,128)S(1)}) custom-call(f32[2,256,256]{2,1,0:T(8,128)S(1)} %copy-done, bf16[8,128,128]{2,1,0:T(8,128)(2,1)S(1)} %bitcast.3, f32[8,128]{1,0:T(8,128)S(1)} %bitcast.4, ...), custom_call_target="tpu_custom_call" | custom-call | tf_op jit(solution)/shard_map/exchange_rim/pallas_call | solution.py:559
  16.8 8.5 %scan_pass.2 = (f32[2,384,384]{2,1,0:T(8,128)S(1)}, f32[9,128,128]{2,1,0:T(8,128)S(1)}) custom-call(s32[8,2]{1,0:T(8,128)S(1)} %copy.10.pos, s32[1,1]{1,0:T(1,128)S(6)} %copy.12.count, f32[2,384,384]{2,1,0:T(8,128)S(1)} %get-tuple-element.14.ext.refs_1_, f32[2,4,128,128]{3,2,1,0:T(8,128)S(1)} %get-tuple-element.15.probe.refs_2_, ...), custom_call_target="tpu_custom_call" | custom-call | tf_op jit(solution)/shard_map/scan_pass/pallas_call | solution.py:156
  25.3 30.0 %exchange_all.1 = (f32[2,384,384]{2,1,0:T(8,128)S(1)}, f32[2,4,128,128]{3,2,1,0:T(8,128)S(1)}) custom-call(f32[2,384,384]{2,1,0:T(8,128)S(1)} %get-tuple-element.18.refs_0_, f32[2,384,384]{2,1,0:T(8,128)S(1)} %get-tuple-element.14.ext.refs_1_, f32[2,4,128,128]{3,2,1,0:T(8,128)S(1)} %get-tuple-element.15.probe.refs_2_, ...), custom_call_target="tpu_custom_call" | custom-call | tf_op jit(solution)/shard_map/exchange_all/pallas_call | solution.py:559
  55.4 8.4 %scan_pass.3 = (f32[2,384,384]{2,1,0:T(8,128)S(1)}, f32[9,128,128]{2,1,0:T(8,128)S(1)}) custom-call(s32[8,2]{1,0:T(8,128)S(1)} %copy.10.pos, s32[1,1]{1,0:T(1,128)S(6)} %copy.12.count, f32[2,384,384]{2,1,0:T(8,128)S(1)} %get-tuple-element.20.ext.refs_1_, f32[2,4,128,128]{3,2,1,0:T(8,128)S(1)} %get-tuple-element.21.probe.refs_2_, ...), custom_call_target="tpu_custom_call" | custom-call | tf_op jit(solution)/shard_map/scan_pass/pallas_call | solution.py:156
  63.8 21.8 %exchange_tile.1 = (f32[2,384,384]{2,1,0:T(8,128)S(1)}, f32[2,4,128,128]{3,2,1,0:T(8,128)S(1)}) custom-call(f32[2,384,384]{2,1,0:T(8,128)S(1)} %get-tuple-element.22.refs_0_, f32[2,384,384]{2,1,0:T(8,128)S(1)} %get-tuple-element.20.ext.refs_1_, f32[2,4,128,128]{3,2,1,0:T(8,128)S(1)} %get-tuple-element.21.probe.refs_2_, ...), custom_call_target="tpu_custom_call" | custom-call | tf_op jit(solution)/shard_map/exchange_tile/pallas_call | solution.py:559
  85.6 1.0 %slice.3 = f32[2,256,256]{2,1,0:T(8,128)} slice(f32[2,384,384]{2,1,0:T(8,128)S(1)} %get-tuple-element.24), slice={[0:2], [64:320], [64:320]} | slice | bytes 1048576 | tf_op jit(solution)/shard_map/slice | solution.py:588
  86.6 0.8 copy.13
Async XLA Ops:
  2.0 1.0 %copy-start = (f32[2,256,256]{2,1,0:T(8,128)S(1)}, f32[2,256,256]{2,1,0:T(8,128)}, u32[]{:S(2)}) copy-start(f32[2,256,256]{2,1,0:T(8,128)} %refs_0_.1) | copy-start | bytes 1572868
  3.1 1.0 %copy-start.1 = (f32[2,4,128,128]{3,2,1,0:T(8,128)S(1)}, f32[2,4,128,128]{3,2,1,0:T(8,128)}, u32[]{:S(2)}) copy-start(f32[2,4,128,128]{3,2,1,0:T(8,128)} %refs_4_.1) | copy-start | bytes 1572868
  4.1 1.0 %copy-start.2 = (bf16[2,2,256,256]{3,2,1,0:T(8,128)(2,1)S(1)}, bf16[2,2,256,256]{3,2,1,0:T(8,128)(2,1)}, u32[]{:S(2)}) copy-start(bf16[2,2,256,256]{3,2,1,0:T(8,128)(2,1)} %constant.2.clone.refs_3_) | copy-start | bytes 1572868
  5.2 0.9 %copy-start.3 = (bf16[1,1,8,128,128]{4,3,2,1,0:T(8,128)(2,1)S(1)}, bf16[1,1,8,128,128]{4,3,2,1,0:T(8,128)(2,1)}, u32[]{:S(2)}) copy-start(bf16[1,1,8,128,128]{4,3,2,1,0:T(8,128)(2,1)} %param.9) | copy-start | bytes 786436
  6.1 0.7 copy-start.4

commit v2 on v1

--- a/solution.py
+++ b/solution.py
@@ -3,32 +3,34 @@
 
 import jax
 import jax.numpy as jnp
-import numpy as np
 from jax import lax
 from jax.experimental import pallas as pl
 from jax.experimental.pallas import tpu as pltpu
 from jax.sharding import PartitionSpec as P
 
 PASSES = 2
-TOGETHER = 2
+TOGETHER = 4
 MESH = pl.DeviceIdType.MESH
 VMEM = pl.BlockSpec(memory_space=pltpu.VMEM)
-HBM = pl.BlockSpec(memory_space=pltpu.HBM)
 SMEM = pl.BlockSpec(memory_space=pltpu.SMEM)
 LIMIT = 48 * 1024 * 1024
 
 
-def dft_tables(length):
-    index = np.arange(length)
-    angle = (index[:, None] * index[None, :] % length) * (2.0 * math.pi / length)
-    cosine, sine = np.cos(angle), np.sin(angle)
-    forward = np.block([[cosine, -sine], [sine, cosine]]).astype(np.float32)
-    inverse = np.block([[cosine, sine], [-sine, cosine]]).astype(np.float32)
-    out = []
-    for table in (forward, inverse):
-        high = table.astype(jnp.bfloat16)
-        out.append(np.stack([high, (table - high.astype(np.float32)).astype(jnp.bfloat16)]))
-    return np.stack(out)
+def write_tables(table, length):
+    first = lax.broadcasted_iota(jnp.int32, (length, length), 0)
+    second = lax.broadcasted_iota(jnp.int32, (length, length), 1)
+    angle = lax.rem(first * second, length).astype(jnp.float32) * (2.0 * math.pi / length)
+    parts = []
+    for value in (jnp.cos(angle), jnp.sin(angle)):
+        high = value.astype(jnp.bfloat16)
+        parts.append((high, (value - high.astype(jnp.float32)).astype(jnp.bfloat16)))
+    for k in range(2):
+        cosine, sine = parts[0][k], parts[1][k]
+        for index, (above, below) in enumerate(((-sine, sine), (sine, -sine))):
+            table[index, k, :length, :length] = cosine
+            table[index, k, :length, length:] = above
+            table[index, k, length:, :length] = below
+            table[index, k, length:, length:] = cosine
 
 
 def split(value, axis):
@@ -57,7 +59,7 @@
     group = 2 if modes % 2 == 0 else 1
     firsts = range(0, modes, group)
     together = wave.shape[0]
-    last = pos.shape[0] - 1
+    last = pos.shape[1] - 1
     tall = pix + 8
     upd[...] = jnp.zeros_like(upd)
     sums[...] = jnp.zeros_like(sums)
@@ -67,7 +69,7 @@
         at = [jnp.minimum(step * together + k, last) for k in range(together)]
         places = []
         for k, p in enumerate(at):
-            row, col = pos[p, 0], pos[p, 1]
+            row, col = pos[0, p], pos[1, p]
             shift, down = lax.rem(col, pix), lax.rem(row, 8)
             rows = pl.ds(pl.multiple_of(row // 8 * 8, 8), tall)
             lanes = pl.ds(pl.multiple_of(col // pix * pix, pix), 2 * pix)
@@ -212,17 +214,8 @@
         (upd, ext, probe, sums, ext_out, probe_out) = refs[:6]
         scratch = refs[6:]
     else:
-        (field_in, patterns_in, scales_in, table, probe, ext_out, amp, table_out, probe_out) = refs[:9]
-        scratch = refs[9:]
-        field, patterns, scales, local = scratch[11:]
-        field_copy = pltpu.make_async_copy(field_in, field, local.at[0])
-        pattern_copy = pltpu.make_async_copy(patterns_in, patterns, local.at[1])
-        scale_copy = pltpu.make_async_copy(scales_in, scales, local.at[2])
-        keep_table = pltpu.make_async_copy(table, table_out, local.at[3])
-        keep_probe = pltpu.make_async_copy(probe, probe_out, local.at[4])
-        field_copy.start()
-        pattern_copy.start()
-        scale_copy.start()
+        (field, ext_out, table_out) = refs[:3]
+        scratch = refs[3:]
     work, low_r, high_r, low_c, high_c, low_s, high_s, send_r, recv_r, send_c, recv_c = scratch[:11]
     full_rows, full_cols = work.shape[1], work.shape[2]
     wide = 2 * rim
@@ -287,7 +280,6 @@
         border = work
         blank = jnp.zeros((field.shape[1], wide), jnp.float32)
         work[...] = jnp.zeros_like(work)
-        field_copy.wait()
         for k in range(2):
             work[k, rim:-rim, :] = pltpu.roll(jnp.concatenate([field[k], blank], 1), rim, 1)
     pl.semaphore_wait(barrier, greeted)
@@ -387,17 +379,9 @@
     if not reduce:
         start_rows()
         begin_cols()
-        keep_table.start()
-        keep_probe.start()
-        pattern_copy.wait()
-        scale_copy.wait()
-        for p in range(amp.shape[0]):
-            column = jnp.broadcast_to(scales[p : p + 1, :], (pix, pix)).T
-            amp[p] = patterns[p].astype(jnp.float32) * column
+        write_tables(table_out, pix)
         finish_rows()
         finish_cols()
-        keep_table.wait()
-        keep_probe.wait()
         drain()
         return
 
@@ -531,15 +515,7 @@
     out = jax.ShapeDtypeStruct(shape, jnp.float32)
     modes = 0
     if kind == "rim":
-        field, patterns, scales, table, probe = operands
-        outs = (
-            out,
-            jax.ShapeDtypeStruct(patterns.shape, jnp.float32),
-            jax.ShapeDtypeStruct(table.shape, table.dtype),
-            jax.ShapeDtypeStruct(probe.shape, jnp.float32),
-        )
-        scratch += [pltpu.VMEM(x.shape, x.dtype) for x in (field, patterns, scales)]
-        scratch.append(pltpu.SemaphoreType.DMA((5,)))
+        outs = (out, jax.ShapeDtypeStruct((2, 2, 2 * pix, 2 * pix), jnp.bfloat16))
     else:
         probe, sums = operands[2:]
         modes = probe.shape[1]
@@ -559,7 +535,7 @@
     return pl.pallas_call(
         functools.partial(exchange_kernel, kind, rim, modes, pix),
         out_shape=outs,
-        in_specs=[HBM if kind == "rim" else VMEM] * len(operands),
+        in_specs=[VMEM] * len(operands),
         out_specs=tuple([VMEM] * len(outs)),
         scratch_shapes=scratch,
         compiler_params=pltpu.CompilerParams(
@@ -572,15 +548,13 @@
 def on_device(object_field, probe, patterns, row_scales, positions, counts):
     modes, pix = probe.shape[1], probe.shape[2]
     rim = pix // 2
-    table = jnp.asarray(dft_tables(pix))
-    starts = positions[0, 0]
+    starts = positions[0, 0].T
+    amp = patterns[0, 0].astype(jnp.float32) * row_scales[0, 0][..., None]
     core, plane, far = col_factors(lax.axis_size("row"), lax.axis_size("col"))
     step = math.lcm(16 * core * max(plane, far), pix)
     rows_padded = -(-(2 * modes + 1) * pix // step) * step
     shape = (2, object_field.shape[1] + pix, object_field.shape[2] + pix)
-    ext, amp, table, probe = exchange(
-        "rim", 0, shape, pix, (object_field, patterns[0, 0], row_scales[0, 0], table, probe)
-    )
+    ext, table = exchange("rim", 0, shape, pix, (object_field,))
     for pass_number in range(PASSES):
         upd, sums = run_pass(ext, probe, amp, starts, counts, table, rows_padded)
         kind = "tile" if pass_number == PASSES - 1 else "all"

time: 87.6 us -> 83.6 us (0.954)
  local copies, waits for them, and re-layouts: 7.3 us -> 2.83 us
  other arithmetic: 0 us -> 1.15 us
  Pallas kernels: 78.8 us -> 77.8 us
    pallas_call x2, Pallas kernels: 16.9 us -> 10.5 us  [run_pass(): pl.pallas_call(pass_kernel, out_shape=(jax.ShapeDtypeStruct(ext.shape, jn...]
    pallas_call x3, Pallas kernels: 61.9 us -> 67.4 us  [exchange(): pl.pallas_call(functools.partial(exchange_kernel, kind, rim, modes, pix),...]
    unnamed x11 -> x7, local copies, waits for them, and re-layouts: 5.55 us -> 1.84 us
    mul x0 -> x1, other arithmetic: none -> 1.15 us  [on_device(): amp = patterns[0, 0].astype(jnp.float32) * row_scales[0, 0][..., None]]
where the time goes in v2:
time: 83.6 us; the launch traced here: 83.2 us
  Pallas kernels  77.8 us (93%)
  local copies, waits for them, and re-layouts  2.83 us (3%)
  between operations  1.42 us (2%)
  other arithmetic  1.15 us (1%)
    pallas_call x3, Pallas kernels, exchange(): pl.pallas_call(functools.partial(exchange_kernel, kind, rim, modes, pix),...  67.4 us
    pallas_call x2, Pallas kernels, run_pass(): pl.pallas_call(pass_kernel, out_shape=(jax.ShapeDtypeStruct(ext.shape, jn...  10.5 us
    unnamed x7, local copies, waits for them, and re-layouts  1.84 us

profile of v2, /device:TPU:0, one launch (start us, length us, event | category | flops | bytes accessed | tf_op | source)
XLA Modules:
  0.0 83.2 jit_solution(16495532856487327047)
XLA Ops:
  0.6 0.0 copy-start
  0.6 0.0 copy-start.2
  1.4 1.2 %convert_multiply_fusion.amp = f32[8,128,128]{2,1,0:T(8,128)S(1)} fusion(bf16[1,1,8,128,128]{4,3,2,1,0:T(8,128)(2,1)} %param.8, f32[8,128]{1,0:T(8,128)} %bitcast.9), kind=kLoop, calls=%fused_computation | loop fusion | flops 262144 | bytes 790528 | tf_op jit(solution)/shard_map/mul | solution.py:552
  2.5 0.0 copy-start.1
  2.5 1.0 %copy-done.1 = f32[2,256,256]{2,1,0:T(8,128)S(1)} copy-done((f32[2,256,256]{2,1,0:T(8,128)S(1)}, f32[2,256,256]{2,1,0:T(8,128)}, u32[]{:S(2)}) %copy-start.1) | copy-done | bytes 524312
  3.6 9.8 %exchange_rim.1 = (f32[2,384,384]{2,1,0:T(8,128)S(1)}, bf16[2,2,256,256]{3,2,1,0:T(8,128)(2,1)S(1)}) custom-call(f32[2,256,256]{2,1,0:T(8,128)S(1)} %copy-done.1), custom_call_target="tpu_custom_call" | custom-call | tf_op jit(solution)/shard_map/exchange_rim/pallas_call | solution.py:535
  13.3 0.0 copy-done
  13.4 0.0 copy-done.2
  13.4 5.2 %scan_pass.2 = (f32[2,384,384]{2,1,0:T(8,128)S(1)}, f32[9,128,128]{2,1,0:T(8,128)S(1)}) custom-call(s32[2,8]{1,0:T(2,128)S(1)} %bitcast.7, s32[1,1]{1,0:T(1,128)S(6)} %copy.9.count, f32[2,384,384]{2,1,0:T(8,128)S(1)} %get-tuple-element.12.ext.refs_1_, f32[2,4,128,128]{3,2,1,0:T(8,128)S(1)} %copy-done, f32[8,128,128]{2,1,0:T(8,128)S(1)} %convert_multiply_fusion.amp, ...), custom_call_target="tpu_custom_call" | custom-call | tf_op jit(solution)/shard_map/scan_pass/pallas_call | solution.py:158
  18.5 32.7 %exchange_all.1 = (f32[2,384,384]{2,1,0:T(8,128)S(1)}, f32[2,4,128,128]{3,2,1,0:T(8,128)S(1)}) custom-call(f32[2,384,384]{2,1,0:T(8,128)S(1)} %get-tuple-element.14.refs_0_, f32[2,384,384]{2,1,0:T(8,128)S(1)} %get-tuple-element.12.ext.refs_1_, f32[2,4,128,128]{3,2,1,0:T(8,128)S(1)} %copy-done, f32[9,128,128]{2,1,0:T(8,128)S(1)} %get-tuple-element.15.refs_3_), custom_call_target="tpu_custom_call" | custom-call | tf_op jit(solution)/shard_map/exchange_all/pallas_call | solution.py:535
  51.3 5.3 %scan_pass.3 = (f32[2,384,384]{2,1,0:T(8,128)S(1)}, f32[9,128,128]{2,1,0:T(8,128)S(1)}) custom-call(s32[2,8]{1,0:T(2,128)S(1)} %bitcast.8, s32[1,1]{1,0:T(1,128)S(6)} %copy.9.count, f32[2,384,384]{2,1,0:T(8,128)S(1)} %get-tuple-element.16.ext.refs_1_, f32[2,4,128,128]{3,2,1,0:T(8,128)S(1)} %get-tuple-element.17.probe.refs_2_, ...), custom_call_target="tpu_custom_call" | custom-call | tf_op jit(solution)/shard_map/scan_pass/pallas_call | solution.py:158
  56.6 24.8 %exchange_tile.1 = (f32[2,384,384]{2,1,0:T(8,128)S(1)}, f32[2,4,128,128]{3,2,1,0:T(8,128)S(1)}) custom-call(f32[2,384,384]{2,1,0:T(8,128)S(1)} %get-tuple-element.18.refs_0_, f32[2,384,384]{2,1,0:T(8,128)S(1)} %get-tuple-element.16.ext.refs_1_, f32[2,4,128,128]{3,2,1,0:T(8,128)S(1)} %get-tuple-element.17.probe.refs_2_, ...), custom_call_target="tpu_custom_call" | custom-call | tf_op jit(solution)/shard_map/exchange_tile/pallas_call | solution.py:535
  81.4 1.0 %slice.3 = f32[2,256,256]{2,1,0:T(8,128)} slice(f32[2,384,384]{2,1,0:T(8,128)S(1)} %get-tuple-element.20), slice={[0:2], [64:320], [64:320]} | slice | bytes 1048576 | tf_op jit(solution)/shard_map/slice | solution.py:562
  82.4 0.8 copy.10
Async XLA Ops:
  0.6 12.7 %copy-start = (f32[2,4,128,128]{3,2,1,0:T(8,128)S(1)}, f32[2,4,128,128]{3,2,1,0:T(8,128)}, u32[]{:S(2)}) copy-start(f32[2,4,128,128]{3,2,1,0:T(8,128)} %refs_2_.1) | copy-start | bytes 1572868
  0.6 12.7 %copy-start.2 = (s32[1,1,8,2]{2,3,1,0:T(2,128)S(1)}, s32[1,1,8,2]{2,3,1,0:T(2,128)}, u32[]{:S(2)}) copy-start(s32[1,1,8,2]{2,3,1,0:T(2,128)} %param.10) | copy-start | bytes 196
  2.5 1.0 %copy-start.1 = (f32[2,256,256]{2,1,0:T(8,128)S(1)}, f32[2,256,256]{2,1,0:T(8,128)}, u32[]{:S(2)}) copy-start(f32[2,256,256]{2,1,0:T(8,128)} %refs_0_.1) | copy-start | bytes 1572868

commit v3 on v2

--- a/solution.py
+++ b/solution.py
@@ -294,16 +294,37 @@
             device_id_type=MESH,
         )
 
-    row_up = copy_to(
-        border.at[:, pl.ds(*send_high), :], low_r, send_r.at[0], recv_r.at[0], {"row": me_row + 1}
-    )
-    row_down = copy_to(
-        border.at[:, pl.ds(*send_low), :], high_r, send_r.at[1], recv_r.at[1], {"row": me_row - 1}
-    )
+    spans_r = [pl.ds(0, wide), pl.ds(full_cols - wide, wide), pl.ds(wide, full_cols - 2 * wide)]
+    row_up, row_down = [], []
+    for j, lanes in enumerate(spans_r):
+        row_up.append(
+            copy_to(
+                border.at[:, pl.ds(*send_high), lanes],
+                low_r.at[:, :, lanes],
+                send_r.at[0, j],
+                recv_r.at[0, j],
+                {"row": me_row + 1},
+            )
+        )
+        row_down.append(
+            copy_to(
+                border.at[:, pl.ds(*send_low), lanes],
+                high_r.at[:, :, lanes],
+                send_r.at[1, j],
+                recv_r.at[1, j],
+                {"row": me_row - 1},
+            )
+        )
 
     def start_rows():
-        pl.when(row_high)(row_up.start)
-        pl.when(row_low)(row_down.start)
+        for j in range(3):
+            pl.when(row_high)(row_up[j].start)
+            pl.when(row_low)(row_down[j].start)
+
+    def add_rows(copies, buffer, put, which):
+        for j in which:
+            copies[j].wait_recv()
+            work[:, pl.ds(*put), spans_r[j]] += buffer[:, :, spans_r[j]]
 
     col_up, col_down = [], []
     for index, (start, length) in enumerate(blocks):
@@ -341,17 +362,17 @@
     def finish_rows():
         @pl.when(row_low)
         def _():
-            row_up.wait_recv()
-            work[:, pl.ds(*put_low), :] += low_r[...]
+            add_rows(row_up, low_r, put_low, (0, 1))
             start_block(0)
 
         @pl.when(row_high)
         def _():
-            row_down.wait_recv()
-            work[:, pl.ds(*put_high), :] += high_r[...]
+            add_rows(row_down, high_r, put_high, (0, 1))
             start_block(2)
 
     def finish_cols():
+        pl.when(row_low)(lambda: add_rows(row_up, low_r, put_low, (2,)))
+        pl.when(row_high)(lambda: add_rows(row_down, high_r, put_high, (2,)))
         ext_out[...] = work[...]
         span = pl.ds(top, sum(put_high) - top)
 
@@ -370,9 +391,9 @@
         pl.when(col_high)(lambda: land(col_down, high_c, full_cols - wide, kind != "tile"))
 
     def drain():
-        pl.when(row_high)(row_up.wait_send)
-        pl.when(row_low)(row_down.wait_send)
         for index in range(3):
+            pl.when(row_high)(row_up[index].wait_send)
+            pl.when(row_low)(row_down[index].wait_send)
             pl.when(col_high)(col_up[index].wait_send)
             pl.when(col_low)(col_down[index].wait_send)
 
@@ -510,8 +531,7 @@
         pltpu.VMEM((2, row_width, full_cols), jnp.float32),
     ]
     scratch += [pltpu.VMEM(side, jnp.float32)] * 4
-    scratch += [pltpu.SemaphoreType.DMA((2,))] * 2
-    scratch += [pltpu.SemaphoreType.DMA((2, 3))] * 2
+    scratch += [pltpu.SemaphoreType.DMA((2, 3))] * 4
     out = jax.ShapeDtypeStruct(shape, jnp.float32)
     modes = 0
     if kind == "rim":

time: 83.6 us -> 82.8 us (level)
  no operation moved by 1% of the time
where the time goes in v3:
time: 82.8 us; the launch traced here: 82.7 us
  Pallas kernels  77.3 us (93%)
  local copies, waits for them, and re-layouts  2.83 us (3%)
  between operations  1.42 us (2%)
  other arithmetic  1.15 us (1%)
    pallas_call x3, Pallas kernels, exchange(): pl.pallas_call(functools.partial(exchange_kernel, kind, rim, modes, pix),...  66.8 us
    pallas_call x2, Pallas kernels, run_pass(): pl.pallas_call(pass_kernel, out_shape=(jax.ShapeDtypeStruct(ext.shape, jn...  10.4 us
    unnamed x7, local copies, waits for them, and re-layouts  1.84 us

profile of v3, /device:TPU:0, one launch (start us, length us, event | category | flops | bytes accessed | tf_op | source)
XLA Modules:
  0.0 82.7 jit_solution(15998259495213725224)
XLA Ops:
  0.6 0.0 copy-start
  0.6 0.0 copy-start.2
  1.4 1.2 %convert_multiply_fusion.amp = f32[8,128,128]{2,1,0:T(8,128)S(1)} fusion(bf16[1,1,8,128,128]{4,3,2,1,0:T(8,128)(2,1)} %param.8, f32[8,128]{1,0:T(8,128)} %bitcast.9), kind=kLoop, calls=%fused_computation | loop fusion | flops 262144 | bytes 790528 | tf_op jit(solution)/shard_map/mul | solution.py:572
  2.5 0.0 copy-start.1
  2.5 1.0 %copy-done.1 = f32[2,256,256]{2,1,0:T(8,128)S(1)} copy-done((f32[2,256,256]{2,1,0:T(8,128)S(1)}, f32[2,256,256]{2,1,0:T(8,128)}, u32[]{:S(2)}) %copy-start.1) | copy-done | bytes 524312
  3.6 9.4 %exchange_rim.1 = (f32[2,384,384]{2,1,0:T(8,128)S(1)}, bf16[2,2,256,256]{3,2,1,0:T(8,128)(2,1)S(1)}) custom-call(f32[2,256,256]{2,1,0:T(8,128)S(1)} %copy-done.1), custom_call_target="tpu_custom_call" | custom-call | tf_op jit(solution)/shard_map/exchange_rim/pallas_call | solution.py:555
  13.0 0.0 copy-done
  13.0 0.0 copy-done.2
  13.0 5.2 %scan_pass.2 = (f32[2,384,384]{2,1,0:T(8,128)S(1)}, f32[9,128,128]{2,1,0:T(8,128)S(1)}) custom-call(s32[2,8]{1,0:T(2,128)S(1)} %bitcast.7, s32[1,1]{1,0:T(1,128)S(6)} %copy.9.count, f32[2,384,384]{2,1,0:T(8,128)S(1)} %get-tuple-element.12.ext.refs_1_, f32[2,4,128,128]{3,2,1,0:T(8,128)S(1)} %copy-done, f32[8,128,128]{2,1,0:T(8,128)S(1)} %convert_multiply_fusion.amp, ...), custom_call_target="tpu_custom_call" | custom-call | tf_op jit(solution)/shard_map/scan_pass/pallas_call | solution.py:158
  18.2 32.2 %exchange_all.1 = (f32[2,384,384]{2,1,0:T(8,128)S(1)}, f32[2,4,128,128]{3,2,1,0:T(8,128)S(1)}) custom-call(f32[2,384,384]{2,1,0:T(8,128)S(1)} %get-tuple-element.14.refs_0_, f32[2,384,384]{2,1,0:T(8,128)S(1)} %get-tuple-element.12.ext.refs_1_, f32[2,4,128,128]{3,2,1,0:T(8,128)S(1)} %copy-done, f32[9,128,128]{2,1,0:T(8,128)S(1)} %get-tuple-element.15.refs_3_), custom_call_target="tpu_custom_call" | custom-call | tf_op jit(solution)/shard_map/exchange_all/pallas_call | solution.py:555
  50.4 5.3 %scan_pass.3 = (f32[2,384,384]{2,1,0:T(8,128)S(1)}, f32[9,128,128]{2,1,0:T(8,128)S(1)}) custom-call(s32[2,8]{1,0:T(2,128)S(1)} %bitcast.8, s32[1,1]{1,0:T(1,128)S(6)} %copy.9.count, f32[2,384,384]{2,1,0:T(8,128)S(1)} %get-tuple-element.16.ext.refs_1_, f32[2,4,128,128]{3,2,1,0:T(8,128)S(1)} %get-tuple-element.17.probe.refs_2_, ...), custom_call_target="tpu_custom_call" | custom-call | tf_op jit(solution)/shard_map/scan_pass/pallas_call | solution.py:158
  55.7 25.2 %exchange_tile.1 = (f32[2,384,384]{2,1,0:T(8,128)S(1)}, f32[2,4,128,128]{3,2,1,0:T(8,128)S(1)}) custom-call(f32[2,384,384]{2,1,0:T(8,128)S(1)} %get-tuple-element.18.refs_0_, f32[2,384,384]{2,1,0:T(8,128)S(1)} %get-tuple-element.16.ext.refs_1_, f32[2,4,128,128]{3,2,1,0:T(8,128)S(1)} %get-tuple-element.17.probe.refs_2_, ...), custom_call_target="tpu_custom_call" | custom-call | tf_op jit(solution)/shard_map/exchange_tile/pallas_call | solution.py:555
  80.9 1.0 %slice.3 = f32[2,256,256]{2,1,0:T(8,128)} slice(f32[2,384,384]{2,1,0:T(8,128)S(1)} %get-tuple-element.20), slice={[0:2], [64:320], [64:320]} | slice | bytes 1048576 | tf_op jit(solution)/shard_map/slice | solution.py:582
  81.9 0.8 copy.10
Async XLA Ops:
  0.6 12.4 %copy-start = (f32[2,4,128,128]{3,2,1,0:T(8,128)S(1)}, f32[2,4,128,128]{3,2,1,0:T(8,128)}, u32[]{:S(2)}) copy-start(f32[2,4,128,128]{3,2,1,0:T(8,128)} %refs_2_.1) | copy-start | bytes 1572868
  0.6 12.4 %copy-start.2 = (s32[1,1,8,2]{2,3,1,0:T(2,128)S(1)}, s32[1,1,8,2]{2,3,1,0:T(2,128)}, u32[]{:S(2)}) copy-start(s32[1,1,8,2]{2,3,1,0:T(2,128)} %param.10) | copy-start | bytes 196
  2.5 1.0 %copy-start.1 = (f32[2,256,256]{2,1,0:T(8,128)S(1)}, f32[2,256,256]{2,1,0:T(8,128)}, u32[]{:S(2)}) copy-start(f32[2,256,256]{2,1,0:T(8,128)} %refs_0_.1) | copy-start | bytes 1572868
